TPU v7x, 256 devices: a whole 4x4x8 slice. The times are simulated.
256 devices in a mesh: ctx: 32 (over x, y, core), head: 8 (over z).
Axes of the slice: x: 4, y: 4, z: 8, core: 2. Of those that a mesh axis runs over, the one named last changes fastest.
Arguments:
- queries: bfloat16 [6144, 8192], P('ctx', 'head'), may hold values from -200 to 200
- key_states: bfloat16 [6144, 1024], P('ctx', 'head'), may hold values from -8 to 8
- value_states: bfloat16 [6144, 1024], P('ctx', 'head'), may hold values from -6 to 6
- head_gates: float32 [64], P('head'), may hold values from 0.1 to 1
- retrieval: int32 [64], P('head'), may hold values 0 or 1
- sink_count: int32 [64], P('head'), may hold values from 1 to 128, as said below
- window_len: int32 [64], P('head'), may hold values from 1024 to 2048, as said below
- out_grad: bfloat16 [6144, 8192], P('ctx', 'head'), may hold values from -6 to 6
Outputs:
- attended: bfloat16 [6144, 8192], P('ctx', 'head')
- grad_queries: bfloat16 [6144, 8192], P('ctx', 'head')
- grad_keys: bfloat16 [6144, 1024], P('ctx', 'head')
- grad_values: bfloat16 [6144, 1024], P('ctx', 'head')
- grad_gates: float32 [64], replicated
Inputs may be any that keep to these rules, and one draw needn't show every extreme that they name: `sink_count`: number of sink tokens of each head; some head has exactly 128 and some head exactly 1. `window_len`: window of each head; some head has exactly 2048 and some head exactly half of 2048.
All inputs are finite; a program needn't handle non-finite values. No bound on the sum of `retrieval` on one device may be relied on, other than what follows from the above.
Results may differ from a plain program's by a relative error of at most 0.04.
Values may be sent and summed in bfloat16 or wider, within the bound.
A program may use at most 128 MiB of HBM per device.

v0:
```python
import math

import jax
import jax.numpy as jnp
from jax import lax
from jax.sharding import PartitionSpec as P

HQ = 64
DH = 128


NEGATIVE = -1e30


def query_mask(query_pos, key_pos, flags, sinks, windows):
    seen = key_pos[None, :] <= query_pos[:, None]
    recent = key_pos[None, :] > query_pos[:, None] - windows[:, :, None, None]
    early = key_pos[None, None, None, :] < sinks[:, :, None, None]
    wide = (flags == 1)[:, :, None, None]
    return seen[None, None] & (wide | early | recent)


def raw_scores(query_part, key_block):
    scale = query_part.shape[-1] ** (-0.5)
    return (
        jnp.einsum("qhgd,khd->hgqk", query_part, key_block, preferred_element_type=jnp.float32)
        * scale
    )


def forward_half(running, query_part, query_pos, key_block, value_block, key_pos, head_info):
    flags, sinks, windows = head_info

    def update(current):
        peak, total, weighted = current
        visible = query_mask(query_pos, key_pos, flags, sinks, windows)
        scores = raw_scores(query_part, key_block)
        fresh = jnp.maximum(peak, jnp.max(jnp.where(visible, scores, NEGATIVE), axis=-1))
        raised = jnp.where(visible, jnp.exp(scores - fresh[..., None]), 0.0)
        carried = jnp.exp(peak - fresh)
        total = total * carried + jnp.sum(raised, axis=-1)
        weighted = weighted * carried[..., None] + jnp.einsum(
            "hgqk,khd->hgqd",
            raised.astype(jnp.bfloat16),
            value_block,
            preferred_element_type=jnp.float32,
        )
        return (fresh, total, weighted)

    def unchanged(current):
        return current

    return lax.cond(key_pos[0] <= jnp.max(query_pos), update, unchanged, running)


def backward_half(
    query_part, query_pos, scaled_grad, log_total, delta, key_block, value_block, key_pos, head_info
):
    flags, sinks, windows = head_info
    scale = query_part.shape[-1] ** (-0.5)

    def compute_grads(unused):
        visible = query_mask(query_pos, key_pos, flags, sinks, windows)
        scores = raw_scores(query_part, key_block)
        probs = jnp.where(visible, jnp.exp(scores - log_total[..., None]), 0.0)
        grad_probs = jnp.einsum(
            "qhgd,khd->hgqk", scaled_grad, value_block, preferred_element_type=jnp.float32
        )
        grad_scores = (probs * (grad_probs - delta[..., None])).astype(jnp.bfloat16)
        results = []
        results.append(
            jnp.einsum("hgqk,khd->qhgd", grad_scores, key_block, preferred_element_type=jnp.float32)
            * scale
        )
        results.append(
            jnp.einsum(
                "hgqk,qhgd->khd", grad_scores, query_part, preferred_element_type=jnp.float32
            )
            * scale
        )
        results.append(
            jnp.einsum(
                "hgqk,qhgd->khd",
                probs.astype(jnp.bfloat16),
                scaled_grad,
                preferred_element_type=jnp.float32,
            )
        )
        return tuple(results)

    def nothing(unused):
        results = []
        results.append(jnp.zeros(query_part.shape, jnp.float32))
        results.append(jnp.zeros(key_block.shape, jnp.float32))
        results.append(jnp.zeros(value_block.shape, jnp.float32))
        return tuple(results)

    return lax.cond(key_pos[0] <= jnp.max(query_pos), compute_grads, nothing, 0)


def local(
    queries, key_states, value_states, head_gates, retrieval, sink_count, window_len, out_grad
):
    rows, width = queries.shape
    kv_local = key_states.shape[1] // DH
    group = width // key_states.shape[1]
    half = rows // 2
    ctx_index = lax.axis_index("ctx")
    head_info = (
        retrieval.reshape(kv_local, group),
        sink_count.reshape(kv_local, group),
        window_len.reshape(kv_local, group),
    )
    gate_grid = head_gates.reshape(kv_local, group)
    paired = jnp.stack([queries, out_grad])
    own_pos = ctx_index * rows + jnp.arange(rows, dtype=jnp.int32)
    query_rows = paired[0].reshape(rows, kv_local, group, DH)
    grad_rows = paired[1].reshape(rows, kv_local, group, DH).astype(jnp.float32)
    query_halves = (query_rows[:half], query_rows[half:])
    pos_halves = (own_pos[:half], own_pos[half:])
    first_state = (
        jnp.full((kv_local, group, half), NEGATIVE, jnp.float32),
        jnp.zeros((kv_local, group, half), jnp.float32),
        jnp.zeros((kv_local, group, half, DH), jnp.float32),
    )
    start_carry = (first_state, first_state)
    key_rows = lax.all_gather(key_states, "ctx", axis=0, tiled=True)
    value_rows = lax.all_gather(value_states, "ctx", axis=0, tiled=True)
    count = key_rows.shape[0]
    span = math.gcd(count, 512)

    def one_block(number, current):
        offset = number * span
        key_block = lax.dynamic_slice_in_dim(key_rows, offset, span, 0).reshape(span, kv_local, DH)
        value_block = lax.dynamic_slice_in_dim(value_rows, offset, span, 0).reshape(
            span, kv_local, DH
        )
        key_pos = offset + jnp.arange(span, dtype=jnp.int32)
        return tuple(
            (
                forward_half(
                    current[part],
                    query_halves[part],
                    pos_halves[part],
                    key_block,
                    value_block,
                    key_pos,
                    head_info,
                )
                for part in range(2)
            )
        )

    finals = lax.fori_loop(0, count // span, one_block, start_carry)
    whole_keys, whole_values = (
        lax.all_gather(key_states, "ctx", axis=0, tiled=True),
        lax.all_gather(value_states, "ctx", axis=0, tiled=True),
    )
    head_out = jnp.concatenate(
        [finals[part][2] / finals[part][1][..., None] for part in range(2)], axis=2
    )
    head_out = head_out.transpose(2, 0, 1, 3)
    log_totals = tuple((finals[part][0] + jnp.log(finals[part][1]) for part in range(2)))
    gate_wide = gate_grid[None, :, :, None]
    attended = (gate_wide * head_out).astype(jnp.bfloat16).reshape(rows, width)
    products = grad_rows * head_out
    gate_part = jnp.sum(products, axis=(0, 3))
    scaled_grad = (gate_wide * grad_rows).astype(jnp.bfloat16)
    delta = (gate_grid[None] * jnp.sum(products, axis=-1)).transpose(1, 2, 0)
    grad_halves = (scaled_grad[:half], scaled_grad[half:])
    delta_halves = (delta[:, :, :half], delta[:, :, half:])
    total_rows = whole_keys.shape[0]
    span_back = math.gcd(total_rows, 512)
    zero_half = jnp.zeros((half, kv_local, group, DH), jnp.float32)

    def block_at(offset, span):
        key_block = lax.dynamic_slice_in_dim(whole_keys, offset, span, 0).reshape(
            span, kv_local, DH
        )
        value_block = lax.dynamic_slice_in_dim(whole_values, offset, span, 0).reshape(
            span, kv_local, DH
        )
        key_pos = offset + jnp.arange(span, dtype=jnp.int32)
        return (key_block, value_block, key_pos)

    def run_half(part, key_block, value_block, key_pos):
        return backward_half(
            query_halves[part],
            pos_halves[part],
            grad_halves[part],
            log_totals[part],
            delta_halves[part],
            key_block,
            value_block,
            key_pos,
            head_info,
        )

    def backward_block(number, running):
        query_grads, key_term, value_term = running
        offset = number * span_back
        key_block, value_block, key_pos = block_at(offset, span_back)
        key_sum = jnp.zeros((span_back, kv_local, DH), jnp.float32)
        value_sum = jnp.zeros((span_back, kv_local, DH), jnp.float32)
        updated = []
        for part in range(2):
            query_add, key_add, value_add = run_half(part, key_block, value_block, key_pos)
            updated.append(query_grads[part] + query_add)
            key_sum = key_sum + key_add
            value_sum = value_sum + value_add
        key_term = lax.dynamic_update_slice_in_dim(key_term, key_sum, offset, 0)
        value_term = lax.dynamic_update_slice_in_dim(value_term, value_sum, offset, 0)
        return (tuple(updated), key_term, value_term)

    zero_term = jnp.zeros((total_rows, kv_local, DH), jnp.float32)
    query_grads, key_term, value_term = lax.fori_loop(
        0, total_rows // span_back, backward_block, ((zero_half, zero_half), zero_term, zero_term)
    )
    key_part, value_part = (
        lax.psum_scatter(
            key_term.reshape(total_rows, kv_local * DH), "ctx", scatter_dimension=0, tiled=True
        ),
        lax.psum_scatter(
            value_term.reshape(total_rows, kv_local * DH), "ctx", scatter_dimension=0, tiled=True
        ),
    )
    grad_queries = jnp.concatenate(query_grads, axis=0).astype(jnp.bfloat16).reshape(rows, width)
    padded = lax.dynamic_update_slice(
        jnp.zeros((HQ,), jnp.float32),
        gate_part.reshape(-1),
        (lax.axis_index("head") * (kv_local * group),),
    )
    grad_gates = lax.psum(padded, ("ctx", "head"))
    return (
        attended,
        grad_queries,
        key_part.astype(jnp.bfloat16),
        value_part.astype(jnp.bfloat16),
        grad_gates,
    )


def solution(mesh):
    return jax.shard_map(
        local,
        mesh=mesh,
        in_specs=(
            P("ctx", "head"),
            P("ctx", "head"),
            P("ctx", "head"),
            P("head"),
            P("head"),
            P("head"),
            P("head"),
            P("ctx", "head"),
        ),
        out_specs=(P("ctx", "head"), P("ctx", "head"), P("ctx", "head"), P("ctx", "head"), P()),
        check_vma=False,
    )
```

profile of v0, /device:TPU:2, one launch (start us, length us, event | category | flops | bytes accessed | tf_op | source)
XLA Modules:
  0.0 565.4 jit_solution(15244047756337095172)
XLA Ops:
  10.9 50.5 %all-gather.3.cloned.1.call-done = bf16[6144,128]{1,0:T(8,128)(2,1)} async-done(((bf16[192,128]{1,0:T(8,128)(2,1)}), bf16[6144,128]{1,0:T(8,128)(2,1)}) %all-gather.3.cloned.1.call-update) | async-done | bytes 1572880 | tf_op jit(solution)/shard_map/all_gather | solution.py:127
  61.5 50.2 %all-gather.5.cloned.1.call-done = bf16[6144,128]{1,0:T(8,128)(2,1)} async-done(((bf16[192,128]{1,0:T(8,128)(2,1)}), bf16[6144,128]{1,0:T(8,128)(2,1)}) %all-gather.5.cloned.1.call-update) | async-done | bytes 1572880 | tf_op jit(solution)/shard_map/all_gather | solution.py:128
  111.8 69.8 %while.45 = (s32[]{:T(128)}, f32[1,8,96]{2,1,0:T(8,128)S(1)}, f32[1,8,96]{2,1,0:T(8,128)S(1)}, f32[1,8,96,128]{3,2,1,0:T(8,128)S(1)}, f32[1,8,96]{2,1,0:T(8,128)...) while((s32[]{:T(128)}, f32[1,8,96]{2,1,0:T(8,128)S(1)}, ...), condition=%wide.region_11.12_spmd, body=%wide.region_2.11_spmd.sunk | while | flops 417323520 | bytes 13025567 | solution.py:154
  115.9 2.5 conditional.10
  118.4 2.5 conditional.11
  125.0 2.5 conditional.10
  127.5 2.5 conditional.11
  134.1 2.5 conditional.10
  136.5 2.5 conditional.11
  143.1 2.5 conditional.10
  145.6 2.5 conditional.11
  183.9 1.9 broadcast_in_dim.50.clone
  187.6 101.5 %while.46 = (s32[]{:T(128)}, f32[96,1,8,128]{3,0,2,1:T(8,128)S(1)}, f32[96,1,8,128]{3,0,2,1:T(8,128)S(1)}, f32[6144,1,128]{2,0,1:T(8,128)}, f32[6144,1,128]{2,0,...) while((s32[]{:T(128)}, f32[96,1,8,128]{3,0,2,1:T(8,128)S(1)}, ...), condition=%wide.region_18.0_spmd.clone, body=%wide.region_13.18_spmd.clone.sunk | while | flops 1015465984 | bytes 23847220 | solution.py:216
  192.5 2.5 conditional.12
  195.1 4.0 conditional.13
  205.2 2.5 conditional.12
  207.7 4.0 conditional.13
  217.8 2.5 conditional.12
  220.3 4.0 conditional.13
  230.4 2.5 conditional.12
  233.0 4.0 conditional.13
  291.5 164.0 %psum.7 = f32[64]{0:T(128)} all-reduce(f32[64]{0:T(128)S(1)} %dynamic_update_slice.19), channel_id=1, replica_groups=mesh['ctx'=32,'head'=8] {'ctx','head'}, use_global_device_ids=true, to_apply=%region_22.23 | all-reduce | flops 64 | bytes 512 | tf_op jit(solution)/shard_map/psum | solution.py:233
  456.3 9.4 %reduce-scatter.5.cloned.1.call-done = f32[192,128]{1,0:T(8,128)} async-done(((f32[6144,128]{1,0:T(8,128)}), f32[192,128]{1,0:T(8,128)}) %reduce-scatter.5.cloned.1.call-update) | async-done | bytes 98320 | tf_op jit(solution)/shard_map/reduce_scatter | solution.py:223
  467.2 90.2 %reduce-scatter.3.cloned.1.call-done = f32[192,128]{1,0:T(8,128)} async-done(((f32[6144,128]{1,0:T(8,128)}), f32[192,128]{1,0:T(8,128)}) %reduce-scatter.3.cloned.1.call-update) | async-done | bytes 98320 | tf_op jit(solution)/shard_map/reduce_scatter | solution.py:220
  (412 shorter events, 122.0 us)
Async XLA Ops:
  7.2 2.8 copy-start.3
  7.2 54.3 %all-gather.3.cloned.1.call-start = ((), (), s32[]{:S(2)}) async-start(), calls=%async_computation.2 | async-start | bytes 1622016 | tf_op jit(solution)/shard_map/all_gather | solution.py:127
  7.9 103.8 %all-gather.5.cloned.1.call-start = ((), (), s32[]{:S(2)}) async-start(), calls=%async_computation.3 | async-start | bytes 1622016 | tf_op jit(solution)/shard_map/all_gather | solution.py:128
  8.7 457.0 %reduce-scatter.5.cloned.1.call-start = ((), (), s32[]{:S(2)}) async-start(), calls=%async_computation.5 | async-start | bytes 3244032 | tf_op jit(solution)/shard_map/reduce_scatter | solution.py:223
  9.9 101.8 %copy-start.4 = (s32[8]{0:T(128)S(1)}, s32[8]{0:T(128)}, u32[]{:S(2)}) copy-start(s32[8]{0:T(128)} %param.25) | copy-start | bytes 100
  10.0 101.8 %copy-start.5 = (s32[8]{0:T(128)S(1)}, s32[8]{0:T(128)}, u32[]{:S(2)}) copy-start(s32[8]{0:T(128)} %param.26) | copy-start | bytes 100
  10.0 101.8 %copy-start.7 = (s32[8]{0:T(128)S(1)}, s32[8]{0:T(128)}, u32[]{:S(2)}) copy-start(s32[8]{0:T(128)} %param.24) | copy-start | bytes 100
  181.6 2.0 copy-start
  181.6 0.7 copy-start.6
  197.3 0.9 copy-start.1
  210.0 0.9 copy-start.1
  222.6 0.9 copy-start.1
  235.2 0.9 copy-start.1
  289.1 268.3 %reduce-scatter.3.cloned.1.call-start = ((), (), s32[]{:S(2)}) async-start(), calls=%async_computation.4 | async-start | bytes 3244032 | tf_op jit(solution)/shard_map/reduce_scatter | solution.py:220
  289.1 1.0 copy-start.2
Sparse Core Ops, SparseCore 0:
  10.6 50.8 all-gather.2
  64.0 47.6 all-gather.4
  289.2 176.3 reduce-scatter.4
  469.9 87.3 reduce-scatter.2
where the time goes:
time: 568 us; the launch traced here: 565 us
  waiting for transfers between devices  202 us (36%)
  blocking collectives  164 us (29%)
  loops' own time  65.2 us (11%)
  local copies, waits for them, and re-layouts  56.9 us (10%)
  matrix products  32.1 us (6%)
  other arithmetic  30.9 us (5%)
  between operations  14.1 us (2%)
    psum x1, blocking collectives, local(): grad_gates = lax.psum(padded, ('ctx', 'head'))  164 us
    reduce_scatter x1, waiting for transfers between devices, local(): lax.psum_scatter(key_term.reshape(total_rows, kv_local * DH), 'ctx', scat...  90.2 us
    all_gather x1, waiting for transfers between devices, local(): key_rows = lax.all_gather(key_states, 'ctx', axis=0, tiled=True)  50.5 us
    all_gather x1, waiting for transfers between devices, local(): value_rows = lax.all_gather(value_states, 'ctx', axis=0, tiled=True)  50.2 us
    another operation x1, loops' own time, local(): finals = lax.fori_loop(0, count // span, one_block, start_carry)  31.7 us
    another operation x1, loops' own time, local(): lax.fori_loop(0, total_rows // span_back, backward_block, ((zero_half, ze...  31.5 us
    dot_general x16, matrix products, raw_scores(): jnp.einsum('qhgd,khd->hgqk', query_part, key_block, preferred_element_typ...  14.2 us
    reshape x12, local copies, waits for them, and re-layouts, one_block(): lax.dynamic_slice_in_dim(value_rows, offset, span, 0)  11.9 us
  transfers between devices with their start and end apart: 4, of which 4 were waited for; matrix products, arithmetic and copies ran while one was open for 1% of the time, Pallas kernels for 0%

commit v1 on v0

v1 whole, which is shorter than its diff:
```python
import math

import jax
import jax.numpy as jnp
from jax import lax
from jax.experimental import pallas as pl
from jax.experimental.pallas import tpu as pltpu
from jax.sharding import PartitionSpec as P

DH = 128
GROUP = 8
ROWS = 192
SEG = 96
STACK = GROUP * SEG
TOKENS = 6144
WIDTH = GROUP * DH
NX = 4
NY = 4
NZ = 8
CTX = NX * NY * 2
BK = 768
SLOTS = TOKENS // BK + 1
RC = 384
NEGATIVE = -1e30
SCALE = DH**-0.5
LOGSCALE = SCALE * math.log2(math.e)
F32 = jnp.float32
BF = jnp.bfloat16
MESH = pl.DeviceIdType.MESH


def dot(a, b, ca, cb):
    return lax.dot_general(a, b, (((ca,), (cb,)), ((), ())), preferred_element_type=F32)


def ctx_of(x, y, c):
    return x * (2 * NY) + y * 2 + c


def loop(count, body):
    def step(n, carry):
        body(n)
        return carry

    lax.fori_loop(0, count, step, 0)


def train_kernel(
    flag_ref, sink_ref, win_ref, gate_ref, q_ref, g_ref, k_ref, v_ref,
    att_out, dq_out, dk_out, dv_out, gg_out,
    k_all, v_all, q_in, g_in, q_s, qt_s, g_s, gt_s, early_s, far_s, late_s, m_s, o_s, d_s, dq_s, s_s, p_s, dkt_s, dvt_s,
    att_s, dqb_s, gg_s, dk_part, dv_part, core_in, kline_in, kline_out, kline_own, klast_in, klast_out,
    vline_in, vline_out, vline_own, vlast_in, vlast_out, gate_in, gate_all,
    own, send_one, recv_one, send_two, recv_two, send_core, recv_core, send_rows, recv_rows,
    send_back, recv_back, send_pair, recv_pair, send_line, recv_line, send_vline, recv_vline,
    send_last, recv_last, send_gate, recv_gate,
):
    me = lax.axis_index("ctx")
    z = lax.axis_index("head")
    x, y, c = me // (2 * NY), (me // 2) % NY, me % 2
    other = {"ctx": ctx_of(x, y, 1 - c)}
    mirror = {"ctx": CTX - 1 - me}
    start0 = me * ROWS
    start1 = (CTX - 1 - me) * ROWS + SEG
    nb0 = start0 // BK + 1
    nb1 = start1 // BK + 1

    def across(d):
        return {"ctx": ctx_of((x + d + 1) % NX, y, c)}

    def along(d):
        return {"ctx": ctx_of(x, (y + d + 1) % NY, c)}

    def heads(d):
        return {"head": (z + d + 1) % NZ}

    def remote(src, dst, send, recv, device):
        return pltpu.make_async_remote_copy(
            src_ref=src, dst_ref=dst, send_sem=send, recv_sem=recv, device_id=device, device_id_type=MESH
        )

    def one_k(d):
        return remote(k_ref, k_all.at[x, y, c], send_one.at[0, d], recv_one.at[0, d], along(d))

    def one_v(d):
        return remote(v_ref, v_all.at[x, y, c], send_one.at[1, d], recv_one.at[1, d], across(d))

    def two_k(d):
        return remote(k_all.at[x, :, c], k_all.at[x, :, c], send_two.at[0, d], recv_two.at[0, d], across(d))

    def two_v(d):
        return remote(v_all.at[:, y, c], v_all.at[:, y, c], send_two.at[1, d], recv_two.at[1, d], along(d))

    def core_k(d):
        at = k_all.at[(x + NX - d) % NX, :, c]
        return remote(at, at, send_core.at[0, d], recv_core.at[0, d], other)

    def core_v(d):
        at = v_all.at[:, (y + NY - d) % NY, c]
        return remote(at, at, send_core.at[1, d], recv_core.at[1, d], other)

    rows_q = remote(q_ref.at[pl.ds(SEG, SEG)], q_in.at[1], send_rows.at[0], recv_rows.at[0], mirror)
    rows_g = remote(g_ref.at[pl.ds(SEG, SEG)], g_in.at[1], send_rows.at[1], recv_rows.at[1], mirror)
    back_att = remote(att_s.at[1], att_out.at[pl.ds(SEG, SEG)], send_back.at[0], recv_back.at[0], mirror)
    back_dq = remote(dqb_s.at[1], dq_out.at[pl.ds(SEG, SEG)], send_back.at[1], recv_back.at[1], mirror)

    def pair_k(n):
        return remote(dk_part.at[(x + n) % NX, :, 1 - c], core_in.at[0, n], send_pair.at[0, n], recv_pair.at[0, n], other)

    def pair_v(n):
        return remote(dv_part.at[(x + n) % NX, :, 1 - c], core_in.at[1, n], send_pair.at[1, n], recv_pair.at[1, n], other)

    def line_k(n):
        return remote(kline_out.at[n - 1], kline_in.at[n - 1], send_line.at[n - 1], recv_line.at[n - 1], across(n - 1))

    def line_v(n, e):
        return remote(vline_out.at[n, e], vline_in.at[n, e], send_vline.at[n, e], recv_vline.at[n, e], along(e))

    def last_k(e):
        return remote(klast_out.at[(y + e + 1) % NY], klast_in.at[e], send_last.at[0, e], recv_last.at[0, e], along(e))

    def last_v(n):
        return remote(vlast_out.at[n - 1], vlast_in.at[n - 1], send_last.at[1, n - 1], recv_last.at[1, n - 1], across(n - 1))

    def gate_copy(n, src, device):
        return remote(src, gate_in.at[n], send_gate.at[n], recv_gate.at[n], device)

    gate_core = gate_copy(0, gg_s, other)
    gate_across = [gate_copy(1 + d, gate_all.at[0], across(d)) for d in range(3)]
    gate_along = [gate_copy(4 + d, gate_all.at[1], along(d)) for d in range(3)]
    gate_heads = [
        remote(gate_all.at[2], gg_out.at[z], send_gate.at[7 + d], recv_gate.at[7 + d], heads(d)) for d in range(NZ - 1)
    ]

    mine = [
        pltpu.make_async_copy(k_ref, k_all.at[x, y, c], own.at[0]),
        pltpu.make_async_copy(v_ref, v_all.at[x, y, c], own.at[1]),
        pltpu.make_async_copy(q_ref.at[pl.ds(0, SEG)], q_in.at[0], own.at[2]),
        pltpu.make_async_copy(g_ref.at[pl.ds(0, SEG)], g_in.at[0], own.at[3]),
    ]
    for copy in mine:
        copy.start()
    greeted = [across(d) for d in range(3)] + [along(d) for d in range(3)] + [other, mirror]
    greeted = greeted + [heads(d) for d in range(NZ - 1)]
    barrier = pltpu.get_barrier_semaphore()
    for device in greeted:
        pl.semaphore_signal(barrier, inc=1, device_id=device, device_id_type=MESH)
    pl.semaphore_wait(barrier, len(greeted))
    for d in range(3):
        one_k(d).start()
        one_v(d).start()

    lane = lax.broadcasted_iota(jnp.int32, (SEG, DH), 1)
    row = lax.broadcasted_iota(jnp.int32, (SEG, DH), 0)

    def prepare(seg):
        start = jnp.where(seg == 0, start0, start1)
        for h in range(GROUP):
            rows = slice(h * SEG, (h + 1) * SEG)
            q_s[seg, rows, :] = q_in[seg, :, h * DH : (h + 1) * DH]
            limit = jnp.where(flag_ref[h] == 1, -1, row + start - win_ref[h])
            far_s[rows, :] = lane - limit
            early_s[rows, :] = lane - sink_ref[h]
            late_s[rows, :] = lane - row - start
        m_s[seg] = jnp.full((STACK, DH), NEGATIVE, F32)
        qt_s[seg] = q_s[seg].T

    def scores(seg, b):
        slot = b + seg * nb0
        last = jnp.where(seg == 0, nb0, nb1) - 1
        base = b * BK
        kb = k_all[b // 2, pl.ds((b % 2) * 2, 2)].reshape(BK, DH)

        def go(full):
            for r in range(0, STACK, RC):
                rows = slice(r, r + RC)
                s = dot(q_s[seg, rows, :], kb, 1, 1)
                best = m_s[seg, rows, :]
                far = far_s[rows, :]
                for t in range(BK // DH):
                    at = base + t * DH
                    seen = far > -at
                    if full:
                        seen = (seen | (early_s[rows, :] < -at)) & (late_s[rows, :] <= -at)
                    part = jnp.where(seen, s[:, t * DH : (t + 1) * DH], NEGATIVE)
                    s_s[slot, rows, t * DH : (t + 1) * DH] = part
                    best = jnp.maximum(best, part)
                m_s[seg, rows, :] = best

        edge = (b == 0) | (b == last)
        pl.when(edge)(lambda: go(True))
        pl.when(jnp.logical_not(edge))(lambda: go(False))

    mine[2].wait()
    mine[0].wait()
    mine[1].wait()
    for d in range(3):
        one_k(d).wait_recv()
        one_v(d).wait_recv()
    for d in range(3):
        two_k(d).start()
        two_v(d).start()
    core_k(0).start()
    core_v(0).start()
    rows_q.start()

    def score_step(step):
        seg = step // 4
        d = step % 4

        @pl.when((step > 0) & (step < 4))
        def _():
            two_k(d - 1).wait_recv()
            core_k(d).start()
            two_v(d - 1).wait_recv()
            core_v(d).start()

        @pl.when(step < 4)
        def _():
            core_k(d).wait_recv()

        @pl.when(step == 4)
        def _():
            rows_q.wait_recv()
            rows_g.start()

        @pl.when(d == 0)
        def _():
            prepare(seg)

        def block(t):
            b = ((x + NX - d) % NX) * 2 + t
            pl.when(b < jnp.where(seg == 0, nb0, nb1))(lambda: scores(seg, b))

        loop(2, block)

    loop(8, score_step)

    def settle(seg):
        peak = jnp.max(m_s[seg], axis=1, keepdims=True)
        m_s[seg] = jnp.broadcast_to(peak * LOGSCALE, (STACK, DH))
        o_s[seg] = jnp.zeros((STACK, 2 * DH), F32)

    loop(2, settle)
    loop(4, lambda d: core_v(d).wait_recv())

    def forward(slot):
        seg = jnp.where(slot < nb0, 0, 1)
        b = slot - seg * nb0
        vb = v_all[b // 2, pl.ds((b % 2) * 2, 2)].reshape(BK, DH)
        vx = jnp.concatenate([vb, jnp.ones((BK, DH), BF)], axis=1)
        for r in range(0, STACK, RC):
            rows = slice(r, r + RC)
            top = m_s[seg, rows, :]
            parts = []
            for t in range(BK // DH):
                part = jnp.exp2(s_s[slot, rows, t * DH : (t + 1) * DH] * LOGSCALE - top).astype(BF)
                p_s[slot, rows, t * DH : (t + 1) * DH] = part
                parts.append(part)
            o_s[seg, rows, :] += dot(jnp.concatenate(parts, axis=1), vx, 1, 0)

    loop(SLOTS, forward)

    mine[3].wait()
    rows_g.wait_recv()
    gg_s[...] = jnp.zeros((GROUP, DH), F32)

    def combine(seg):
        for h in range(GROUP):
            rows = slice(h * SEG, (h + 1) * SEG)
            columns = slice(h * DH, (h + 1) * DH)
            share = 1.0 / o_s[seg, rows, DH:]
            out = o_s[seg, rows, :DH] * share
            att_s[seg, :, columns] = (gate_ref[h] * out).astype(BF)
            grad = g_in[seg, :, columns].astype(F32)
            by_row = jnp.sum(grad * out, axis=1, keepdims=True)
            gg_s[h : h + 1, :] += jnp.broadcast_to(jnp.sum(by_row, axis=0, keepdims=True), (1, DH))
            weight = gate_ref[h] * share
            d_s[seg, rows, :] = by_row * weight
            g_s[seg, rows, :] = (grad * weight).astype(BF)
        gt_s[seg] = g_s[seg].T
        dq_s[seg] = jnp.zeros((STACK, DH), F32)

    loop(2, combine)
    keep_att = pltpu.make_async_copy(att_s.at[0], att_out.at[pl.ds(0, SEG)], own.at[4])
    keep_dq = pltpu.make_async_copy(dqb_s.at[0], dq_out.at[pl.ds(0, SEG)], own.at[5])
    keep_att.start()
    back_att.start()
    gate_core.start()

    def backward(seg, b, t):
        slot = b + seg * nb0
        kb = k_all[b // 2, pl.ds(t * 2, 2)].reshape(BK, DH)
        vb = v_all[b // 2, pl.ds(t * 2, 2)].reshape(BK, DH)
        dp = dot(g_s[seg], vb, 1, 1)
        delta = d_s[seg]
        p = p_s[slot]
        ds = jnp.concatenate(
            [p[:, i : i + DH] * (dp[:, i : i + DH] - delta).astype(BF) for i in range(0, BK, DH)], axis=1
        )
        dq_s[seg] += dot(ds, kb, 1, 0)
        dkt_s[t] += dot(qt_s[seg], ds, 1, 0)
        dvt_s[t] += dot(gt_s[seg], p, 1, 0)

    def write_dq(seg):
        for h in range(GROUP):
            dqb_s[seg, :, h * DH : (h + 1) * DH] = (dq_s[seg, h * SEG : (h + 1) * SEG, :] * SCALE).astype(BF)

    def spread_v(n):
        at = (x + n) % NX
        vline_own[n] = dv_part[at, y, c].astype(F32) + core_in[1, n, y].astype(F32)
        for e in range(3):
            to = (y + e + 1) % NY
            vline_out[n, e] = (dv_part[at, to, c].astype(F32) + core_in[1, n, to].astype(F32)).astype(BF)
            line_v(n, e).start()

    def sum_v(n):
        for e in range(3):
            line_v(n, e).wait_recv()
        total = vline_own[n]
        for e in range(3):
            total = total + vline_in[n, e].astype(F32)
        return total

    def gate_step(step):
        @pl.when(step == 0)
        def _():
            gate_core.wait_recv()
            gate_all[0] = gg_s[...] + gate_in[0]
            for copy in gate_across:
                copy.start()

        @pl.when(step == 1)
        def _():
            for copy in gate_across:
                copy.wait_recv()
            gate_all[1] = gate_all[0] + gate_in[1] + gate_in[2] + gate_in[3]
            for copy in gate_along:
                copy.start()

        @pl.when(step == 2)
        def _():
            for copy in gate_along:
                copy.wait_recv()
            total = gate_all[1] + gate_in[4] + gate_in[5] + gate_in[6]
            gate_all[2] = total
            gg_out[z] = total
            for copy in gate_heads:
                copy.start()

    def grad_step(step):
        n = (step + 1) % NX
        at = (x + n) % NX
        dkt_s[...] = jnp.zeros((2, DH, BK), F32)
        dvt_s[...] = jnp.zeros((2, DH, BK), F32)

        def turn(index):
            seg = 1 - index

            def block(t):
                b = at * 2 + t
                pl.when(b < jnp.where(seg == 0, nb0, nb1))(lambda: backward(seg, b, t))

            loop(2, block)

            @pl.when((step == 3) & (index == 0))
            def _():
                write_dq(1)
                back_dq.start()

        loop(2, turn)
        for t in range(2):
            dk_part[at, t * 2 : t * 2 + 2] = (dkt_s[t] * SCALE).T.astype(BF).reshape(2, 2, ROWS, DH)
            dv_part[at, t * 2 : t * 2 + 2] = dvt_s[t].T.astype(BF).reshape(2, 2, ROWS, DH)
        pair_k(n).start()
        pair_v(n).start()
        gate_step(step)

        @pl.when(step > 0)
        def _():
            pair_k(step).wait_recv()
            group = (x + step) % NX
            kline_out[step - 1] = (dk_part[group, :, c].astype(F32) + core_in[0, step].astype(F32)).astype(BF)
            line_k(step).start()
            pair_v(step).wait_recv()
            spread_v(step)

        @pl.when(step > 1)
        def _():
            vlast_out[step - 2] = sum_v(step - 1).astype(BF)
            last_v(step - 1).start()

    loop(4, grad_step)
    write_dq(0)
    keep_dq.start()

    pair_v(0).wait_recv()
    spread_v(0)
    pair_k(0).wait_recv()
    kline_own[...] = dk_part[x, :, c].astype(F32) + core_in[0, 0].astype(F32)
    for n in range(1, 4):
        line_k(n).wait_recv()
    kline_own[...] += kline_in[0].astype(F32) + kline_in[1].astype(F32) + kline_in[2].astype(F32)
    klast_out[...] = kline_own[...].astype(BF)
    for e in range(3):
        last_k(e).start()
    vlast_out[2] = sum_v(3).astype(BF)
    last_v(3).start()
    v_total = sum_v(0)
    k_total = kline_own[y]
    for e in range(3):
        last_k(e).wait_recv()
        k_total = k_total + klast_in[e].astype(F32)
    dk_out[...] = k_total.astype(BF)
    for n in range(1, 4):
        last_v(n).wait_recv()
        v_total = v_total + vlast_in[n - 1].astype(F32)
    dv_out[...] = v_total.astype(BF)
    for copy in gate_heads:
        copy.wait_recv()
    keep_att.wait()
    keep_dq.wait()
    back_att.wait()
    back_dq.wait()
    rows_q.wait_send()
    rows_g.wait_send()
    for d in range(3):
        one_k(d).wait_send()
        one_v(d).wait_send()
        two_k(d).wait_send()
        two_v(d).wait_send()
        line_k(d + 1).wait_send()
        last_k(d).wait_send()
        last_v(d + 1).wait_send()
    for n in range(4):
        core_k(n).wait_send()
        core_v(n).wait_send()
        pair_k(n).wait_send()
        pair_v(n).wait_send()
        for e in range(3):
            line_v(n, e).wait_send()
    for copy in [gate_core] + gate_across + gate_along + gate_heads:
        copy.wait_send()


def train(flags, sinks, wins, gates, q, g, k, v):
    smem = pl.BlockSpec(memory_space=pltpu.SMEM)
    vmem = pl.BlockSpec(memory_space=pltpu.VMEM)
    anywhere = pl.BlockSpec(memory_space=pl.ANY)
    dma = pltpu.SemaphoreType.DMA
    shape = jax.ShapeDtypeStruct
    hold = pltpu.VMEM
    whole = (NX, NY, 2, ROWS, DH)
    block = (NY, ROWS, DH)
    return pl.pallas_call(
        train_kernel,
        out_shape=(
            shape((ROWS, WIDTH), BF), shape((ROWS, WIDTH), BF), shape((ROWS, DH), BF), shape((ROWS, DH), BF),
            shape((NZ, GROUP, DH), F32),
        ),
        in_specs=[smem] * 4 + [anywhere] * 4,
        out_specs=[anywhere] * 2 + [vmem] * 3,
        scratch_shapes=[
            hold(whole, BF), hold(whole, BF), hold((2, SEG, WIDTH), BF), hold((2, SEG, WIDTH), BF),
            hold((2, STACK, DH), BF), hold((2, DH, STACK), BF), hold((2, STACK, DH), BF), hold((2, DH, STACK), BF),
            hold((STACK, DH), jnp.int32), hold((STACK, DH), jnp.int32), hold((STACK, DH), jnp.int32),
            hold((2, STACK, DH), F32), hold((2, STACK, 2 * DH), F32), hold((2, STACK, DH), F32), hold((2, STACK, DH), F32),
            hold((SLOTS, STACK, BK), F32), hold((SLOTS, STACK, BK), BF), hold((2, DH, BK), F32), hold((2, DH, BK), F32),
            hold((2, SEG, WIDTH), BF), hold((2, SEG, WIDTH), BF), hold((GROUP, DH), F32),
            hold(whole, BF), hold(whole, BF), hold((2, 4) + block, BF),
            hold((3,) + block, BF), hold((3,) + block, BF), hold(block, F32), hold((3, ROWS, DH), BF), hold(block, BF),
            hold((4, 3, ROWS, DH), BF), hold((4, 3, ROWS, DH), BF), hold((4, ROWS, DH), F32),
            hold((3, ROWS, DH), BF), hold((3, ROWS, DH), BF),
            hold((7, GROUP, DH), F32), hold((3, GROUP, DH), F32),
            dma((6,)), dma((2, 3)), dma((2, 3)), dma((2, 3)), dma((2, 3)), dma((2, 4)), dma((2, 4)), dma((2,)), dma((2,)),
            dma((2,)), dma((2,)), dma((2, 4)), dma((2, 4)), dma((3,)), dma((3,)), dma((4, 3)), dma((4, 3)),
            dma((2, 3)), dma((2, 3)), dma((14,)), dma((14,)),
        ],
        compiler_params=pltpu.CompilerParams(
            collective_id=0, has_side_effects=True, vmem_limit_bytes=60 * 1024 * 1024
        ),
        name="train",
    )(flags, sinks, wins, gates, q, g, k, v)


def local(queries, key_states, value_states, head_gates, retrieval, sink_count, window_len, out_grad):
    att, dq, dk, dv, gg = train(
        retrieval, sink_count, window_len, head_gates, queries, out_grad, key_states, value_states
    )
    return att, dq, dk, dv, gg[:, :, 0].reshape(NZ * GROUP)


def solution(mesh):
    wide = P("ctx", "head")
    return jax.shard_map(
        local,
        mesh=mesh,
        in_specs=(wide, wide, wide, P("head"), P("head"), P("head"), P("head"), wide),
        out_specs=(wide, wide, wide, wide, P()),
        check_vma=False,
    )
```

time: 568 us -> 80.8 us (0.14)
  waiting for transfers between devices: 202 us -> 0 us
  blocking collectives: 164 us -> 0 us
  Pallas kernels: 0 us -> 74.3 us
  loops' own time: 65.2 us -> 0 us
  local copies, waits for them, and re-layouts: 56.9 us -> 5.49 us
  matrix products: 32.1 us -> 0 us
  other arithmetic: 30.9 us -> 0 us
  between operations: 14.1 us -> 0.65 us
    psum x1 -> x0, blocking collectives: 164 us -> none  [local(): grad_gates = lax.psum(padded, ('ctx', 'head'))]
    all_gather x2 -> x0, waiting for transfers between devices: 101 us -> none  [the longest x1 50.5 us: local(): key_rows = lax.all_gather(key_states, 'ctx', axis=0, tiled=True)]
    reduce_scatter x2 -> x0, waiting for transfers between devices: 99.6 us -> none  [the longest x1 90.2 us: local(): lax.psum_scatter(key_term.reshape(total_rows, kv_local * DH), 'ctx', scat...]
    pallas_call x0 -> x1, Pallas kernels: none -> 74.3 us  [train(): pl.pallas_call(train_kernel, out_shape=(shape((ROWS, WIDTH), BF), shape((...]
    another operation x50 -> x0, loops' own time: 65.2 us -> none  [the longest x1 31.7 us: local(): finals = lax.fori_loop(0, count // span, one_block, start_carry)]
    reshape x36 -> x0, local copies, waits for them, and re-layouts: 34 us -> none  [the longest x12 11.9 us: one_block(): lax.dynamic_slice_in_dim(value_rows, offset, span, 0)]
    dot_general x56 -> x0, matrix products: 32.1 us -> none  [the longest x16 14.2 us: raw_scores(): jnp.einsum('qhgd,khd->hgqk', query_part, key_block, preferred_element_typ...]
    slice x26 -> x1, local copies, waits for them, and re-layouts: 12.4 us -> 0.84 us  [local(): return (att, dq, dk, dv, gg[:, :, 0].reshape(NZ * GROUP))]
  transfers between devices with their start and end apart: 4 -> 0, of which waited for: 4 -> 0; matrix products, arithmetic and copies ran while one was open for 1% -> 0% of each run, Pallas kernels for 0% -> 0%
where the time goes in v1:
time: 80.8 us; the launch traced here: 80.5 us
  Pallas kernels  74.3 us (92%)
  local copies, waits for them, and re-layouts  5.49 us (7%)
    pallas_call x1, Pallas kernels, train(): pl.pallas_call(train_kernel, out_shape=(shape((ROWS, WIDTH), BF), shape((...  74.3 us
    unnamed x10, local copies, waits for them, and re-layouts  4.05 us

profile of v1, /device:TPU:2, one launch (start us, length us, event | category | flops | bytes accessed | tf_op | source)
XLA Modules:
  0.0 80.5 jit_solution(17497271379870370583)
XLA Ops:
  0.6 74.3 %train.1 = (bf16[192,1024]{1,0:T(8,128)(2,1)}, bf16[192,1024]{1,0:T(8,128)(2,1)}, bf16[192,128]{1,0:T(8,128)(2,1)}, bf16[192,128]{1,0:T(8,128)(2,1)}, f32[8,8,128]{2,1,0:T(8,128)}) custom-call(s32[8]{0:T(128)} %flag_ref.1, s32[8]{0:T(128)} %sink_ref.1, s32[8]{0:T(128)} %win_ref.1, f32[8]{0:T(128)} %gate_ref.1, bf16[192,1024]{1,0:T(8,128)(2,1)} %q_ref.1, ...), custom_call_target="tpu_custom_call" | custom-call | tf_op jit(solution)/shard_map/train/pallas_call | solution.py:455
  75.0 0.8 %slice_reduce_fusion = f32[8,8]{1,0:T(8,128)S(1)} fusion(f32[8,8,128]{2,1,0:T(8,128)} %get-tuple-element.14), kind=kLoop, calls=%fused_computation | loop fusion | bytes 512 | tf_op jit(solution)/shard_map/slice | solution.py:490
  75.8 0.6 reshape_squeeze.3
  76.4 0.0 copy-start
  76.4 1.8 %copy.17 = bf16[192,1024]{1,0:T(8,128)(2,1)} copy(bf16[192,1024]{1,0:T(8,128)(2,1)} %get-tuple-element.20) | data formatting | bytes 786432
  78.2 0.0 copy-done
  78.2 0.0 copy-start.2
  78.2 0.7 copy.18
  79.0 0.1 copy-done.2
  79.0 0.0 copy-start.1
  79.0 0.6 copy.19
  79.7 0.2 copy-done.1
  79.9 0.6 copy.20
Async XLA Ops:
  76.4 1.8 %copy-start = (bf16[192,1024]{1,0:T(8,128)(2,1)S(1)}, bf16[192,1024]{1,0:T(8,128)(2,1)}, u32[]{:S(2)}) copy-start(bf16[192,1024]{1,0:T(8,128)(2,1)} %get-tuple-element.21) | copy-start | bytes 1179652
  78.2 0.8 copy-start.2
  79.0 0.8 %copy-start.1 = (bf16[192,128]{1,0:T(8,128)(2,1)S(1)}, bf16[192,128]{1,0:T(8,128)(2,1)}, u32[]{:S(2)}) copy-start(bf16[192,128]{1,0:T(8,128)(2,1)} %get-tuple-element.23) | copy-start | bytes 147460

commit v2 on v1

v2 whole, which is shorter than its diff:
```python
import math

import jax
import jax.numpy as jnp
from jax import lax
from jax.experimental import pallas as pl
from jax.experimental.pallas import tpu as pltpu
from jax.sharding import PartitionSpec as P

DH = 128
GROUP = 8
ROWS = 192
MOVE = 48
SEGS = (ROWS - MOVE, MOVE)
STACKS = (GROUP * SEGS[0], GROUP * SEGS[1])
UNIT = GROUP * MOVE
UNITS = tuple(n // UNIT for n in STACKS)
TOKENS = 6144
WIDTH = GROUP * DH
NX = 4
NY = 4
NZ = 8
CTX = NX * NY * 2
BK = 768
BLOCKS = TOKENS // BK
SLOTS = BLOCKS * UNITS[0] + UNITS[1]
NEGATIVE = -1e30
SCALE = DH**-0.5
LOGSCALE = SCALE * math.log2(math.e)
F32 = jnp.float32
BF = jnp.bfloat16
MESH = pl.DeviceIdType.MESH


def dot(a, b, ca, cb):
    return lax.dot_general(a, b, (((ca,), (cb,)), ((), ())), preferred_element_type=F32)


def ctx_of(x, y, c):
    return x * (2 * NY) + y * 2 + c


def loop(count, body):
    def step(n, carry):
        body(n)
        return carry

    lax.fori_loop(0, count, step, 0)


def train_kernel(
    flag_ref, sink_ref, win_ref, gate_ref, q_ref, g_ref, k_ref, v_ref,
    att_out, dq_out, dk_out, dv_out, gg_out,
    k_all, v_all, q_in0, q_in1, g_in0, g_in1, q_s0, q_s1, qt_s0, qt_s1, g_s0, g_s1, gt_s0, gt_s1,
    early_s0, early_s1, far_s0, far_s1, late_s0, late_s1, m_s0, m_s1, o_s0, o_s1, d_s0, d_s1, dq_s0, dq_s1, s_s, dkt_s, dvt_s,
    att_s0, att_s1, dqb_s0, dqb_s1, gg_s, dk_part, dv_part, core_in, kline_in, kline_out, kline_own, klast_in, klast_out,
    vline_in, vline_out, vline_own, vlast_in, vlast_out, gate_in, gate_all,
    own, send_one, recv_one, send_two, recv_two, send_core, recv_core, send_rows, recv_rows,
    send_back, recv_back, send_pair, recv_pair, send_line, recv_line, send_vline, recv_vline,
    send_last, recv_last, send_gate, recv_gate,
):
    q_in, g_in, q_s, qt_s, g_s, gt_s = (q_in0, q_in1), (g_in0, g_in1), (q_s0, q_s1), (qt_s0, qt_s1), (g_s0, g_s1), (gt_s0, gt_s1)
    early_s, far_s, late_s = (early_s0, early_s1), (far_s0, far_s1), (late_s0, late_s1)
    m_s, o_s, d_s, dq_s, att_s, dqb_s = (m_s0, m_s1), (o_s0, o_s1), (d_s0, d_s1), (dq_s0, dq_s1), (att_s0, att_s1), (dqb_s0, dqb_s1)
    me = lax.axis_index("ctx")
    z = lax.axis_index("head")
    x, y, c = me // (2 * NY), (me // 2) % NY, me % 2
    other = {"ctx": ctx_of(x, y, 1 - c)}
    mirror = {"ctx": CTX - 1 - me}
    start0 = me * ROWS
    start1 = (CTX - 1 - me) * ROWS + SEGS[0]
    nb0 = start0 // BK + 1
    nb1 = start1 // BK + 1
    starts = (start0, start1)
    blocks = (nb0, nb1)
    bases = (0, nb0 * UNITS[0])

    def across(d):
        return {"ctx": ctx_of((x + d + 1) % NX, y, c)}

    def along(d):
        return {"ctx": ctx_of(x, (y + d + 1) % NY, c)}

    def heads(d):
        return {"head": (z + d + 1) % NZ}

    def remote(src, dst, send, recv, device):
        return pltpu.make_async_remote_copy(
            src_ref=src, dst_ref=dst, send_sem=send, recv_sem=recv, device_id=device, device_id_type=MESH
        )

    def one_k(d):
        return remote(k_ref, k_all.at[x, y, c], send_one.at[0, d], recv_one.at[0, d], along(d))

    def one_v(d):
        return remote(v_ref, v_all.at[x, y, c], send_one.at[1, d], recv_one.at[1, d], across(d))

    def two_k(d, j):
        at = k_all.at[x, (y + NY - j) % NY, c]
        return remote(at, at, send_two.at[0, d, j], recv_two.at[0, d, j], across(d))

    def two_v(d, j):
        at = v_all.at[(x + NX - j) % NX, y, c]
        return remote(at, at, send_two.at[1, d, j], recv_two.at[1, d, j], along(d))

    def core_k(d):
        at = k_all.at[(x + NX - d) % NX, :, c]
        return remote(at, at, send_core.at[0, d], recv_core.at[0, d], other)

    def core_v(d):
        at = v_all.at[:, (y + NY - d) % NY, c]
        return remote(at, at, send_core.at[1, d], recv_core.at[1, d], other)

    rows_q = remote(q_ref.at[pl.ds(SEGS[0], MOVE)], q_in[1], send_rows.at[0], recv_rows.at[0], mirror)
    rows_g = remote(g_ref.at[pl.ds(SEGS[0], MOVE)], g_in[1], send_rows.at[1], recv_rows.at[1], mirror)
    back_att = remote(att_s[1], att_out.at[pl.ds(SEGS[0], MOVE)], send_back.at[0], recv_back.at[0], mirror)
    back_dq = remote(dqb_s[1], dq_out.at[pl.ds(SEGS[0], MOVE)], send_back.at[1], recv_back.at[1], mirror)

    def pair_k(n):
        return remote(dk_part.at[(x + n) % NX, :, 1 - c], core_in.at[0, n], send_pair.at[0, n], recv_pair.at[0, n], other)

    def pair_v(n):
        return remote(dv_part.at[(x + n) % NX, :, 1 - c], core_in.at[1, n], send_pair.at[1, n], recv_pair.at[1, n], other)

    def line_k(n):
        return remote(kline_out.at[n - 1], kline_in.at[n - 1], send_line.at[n - 1], recv_line.at[n - 1], across(n - 1))

    def line_v(n, e):
        return remote(vline_out.at[n, e], vline_in.at[n, e], send_vline.at[n, e], recv_vline.at[n, e], along(e))

    def last_k(e):
        return remote(klast_out.at[(y + e + 1) % NY], klast_in.at[e], send_last.at[0, e], recv_last.at[0, e], along(e))

    def last_v(n):
        return remote(vlast_out.at[n - 1], vlast_in.at[n - 1], send_last.at[1, n - 1], recv_last.at[1, n - 1], across(n - 1))

    def gate_copy(n, src, device):
        return remote(src, gate_in.at[n], send_gate.at[n], recv_gate.at[n], device)

    gate_core = gate_copy(0, gg_s, other)
    gate_across = [gate_copy(1 + d, gate_all.at[0], across(d)) for d in range(3)]
    gate_along = [gate_copy(4 + d, gate_all.at[1], along(d)) for d in range(3)]
    gate_heads = [
        remote(gate_all.at[2], gate_in.at[7 + d], send_gate.at[7 + d], recv_gate.at[7 + d], heads(d)) for d in range(NZ - 1)
    ]

    mine = [
        pltpu.make_async_copy(k_ref, k_all.at[x, y, c], own.at[0]),
        pltpu.make_async_copy(v_ref, v_all.at[x, y, c], own.at[1]),
        pltpu.make_async_copy(q_ref.at[pl.ds(0, SEGS[0])], q_in[0], own.at[2]),
        pltpu.make_async_copy(g_ref.at[pl.ds(0, SEGS[0])], g_in[0], own.at[3]),
    ]
    for copy in mine:
        copy.start()
    greeted = [across(d) for d in range(3)] + [along(d) for d in range(3)] + [other, mirror]
    greeted = greeted + [heads(d) for d in range(NZ - 1)]
    barrier = pltpu.get_barrier_semaphore()
    for device in greeted:
        pl.semaphore_signal(barrier, inc=1, device_id=device, device_id_type=MESH)
    pl.semaphore_wait(barrier, len(greeted))
    for d in range(3):
        one_k(d).start()
        one_v(d).start()
    mine[0].wait()
    mine[1].wait()
    for d in range(3):
        two_k(d, 0).start()
        two_v(d, 0).start()

    def prepare(seg):
        size = SEGS[seg]
        lane = lax.broadcasted_iota(jnp.int32, (size, DH), 1)
        row = lax.broadcasted_iota(jnp.int32, (size, DH), 0)
        for h in range(GROUP):
            rows = slice(h * size, (h + 1) * size)
            q_s[seg][rows, :] = q_in[seg][:, h * DH : (h + 1) * DH]
            limit = jnp.where(flag_ref[h] == 1, -1, row + starts[seg] - win_ref[h])
            far_s[seg][rows, :] = lane - limit
            early_s[seg][rows, :] = lane - sink_ref[h]
            late_s[seg][rows, :] = lane - row - starts[seg]
        m_s[seg][...] = jnp.full((STACKS[seg], DH), NEGATIVE, F32)
        qt_s[seg][...] = q_s[seg][...].T

    def scores(seg, b):
        base = b * BK
        kb = k_all[b // 2, pl.ds((b % 2) * 2, 2)].reshape(BK, DH)

        def go(full):
            for u in range(UNITS[seg]):
                rows = slice(u * UNIT, (u + 1) * UNIT)
                slot = bases[seg] + b * UNITS[seg] + u
                s = dot(q_s[seg][rows, :], kb, 1, 1)
                best = m_s[seg][rows, :]
                far = far_s[seg][rows, :]
                for t in range(BK // DH):
                    at = base + t * DH
                    seen = far > -at
                    if full:
                        seen = (seen | (early_s[seg][rows, :] < -at)) & (late_s[seg][rows, :] <= -at)
                    part = jnp.where(seen, s[:, t * DH : (t + 1) * DH], NEGATIVE)
                    s_s[slot, :, t * DH : (t + 1) * DH] = part
                    best = jnp.maximum(best, part)
                m_s[seg][rows, :] = best

        edge = (b == 0) | (b == blocks[seg] - 1)
        pl.when(edge)(lambda: go(True))
        pl.when(jnp.logical_not(edge))(lambda: go(False))

    for j in range(1, 4):
        one_k(j - 1).wait_recv()
        one_v(j - 1).wait_recv()
        for d in range(3):
            two_k(d, j).start()
            two_v(d, j).start()
    mine[2].wait()
    core_k(0).start()
    core_v(0).start()
    rows_q.start()

    prepare(0)

    def score_step(d):
        @pl.when(d > 0)
        def _():
            for j in range(4):
                two_k(d - 1, j).wait_recv()
            core_k(d).start()
            for j in range(4):
                two_v(d - 1, j).wait_recv()
            core_v(d).start()

        core_k(d).wait_recv()

        def block(t):
            b = ((x + NX - d) % NX) * 2 + t
            pl.when(b < nb0)(lambda: scores(0, b))

        loop(2, block)

    loop(4, score_step)
    rows_q.wait_recv()
    rows_g.start()
    prepare(1)
    loop(nb1, lambda b: scores(1, b))
    for seg in range(2):
        peak = jnp.max(m_s[seg][...], axis=1, keepdims=True)
        m_s[seg][...] = jnp.broadcast_to(peak * LOGSCALE, (STACKS[seg], DH))
        o_s[seg][...] = jnp.zeros((STACKS[seg], 2 * DH), F32)
    loop(4, lambda d: core_v(d).wait_recv())

    def forward(seg, b):
        vb = v_all[b // 2, pl.ds((b % 2) * 2, 2)].reshape(BK, DH)
        vx = jnp.concatenate([vb, jnp.ones((BK, DH), BF)], axis=1)
        for u in range(UNITS[seg]):
            rows = slice(u * UNIT, (u + 1) * UNIT)
            slot = bases[seg] + b * UNITS[seg] + u
            top = m_s[seg][rows, :]
            parts = []
            for t in range(BK // DH):
                part = jnp.exp2(s_s[slot, :, t * DH : (t + 1) * DH] * LOGSCALE - top)
                s_s[slot, :, t * DH : (t + 1) * DH] = part
                parts.append(part.astype(BF))
            o_s[seg][rows, :] += dot(jnp.concatenate(parts, axis=1), vx, 1, 0)

    loop(nb0, lambda b: forward(0, b))
    loop(nb1, lambda b: forward(1, b))

    mine[3].wait()
    rows_g.wait_recv()
    spot = lax.broadcasted_iota(jnp.int32, (8, DH), 1) - z * GROUP
    gg_s[...] = jnp.zeros((8, DH), F32)

    for seg in range(2):
        size = SEGS[seg]
        for h in range(GROUP):
            rows = slice(h * size, (h + 1) * size)
            columns = slice(h * DH, (h + 1) * DH)
            share = 1.0 / o_s[seg][rows, DH:]
            out = o_s[seg][rows, :DH] * share
            att_s[seg][:, columns] = (gate_ref[h] * out).astype(BF)
            grad = g_in[seg][:, columns].astype(F32)
            by_row = jnp.sum(grad * out, axis=1, keepdims=True)
            gg_s[...] += jnp.where(spot == h, jnp.sum(by_row, axis=0, keepdims=True), 0.0)
            weight = gate_ref[h] * share
            d_s[seg][rows, :] = by_row * weight
            g_s[seg][rows, :] = (grad * weight).astype(BF)
        gt_s[seg][...] = g_s[seg][...].T
        dq_s[seg][...] = jnp.zeros((STACKS[seg], DH), F32)

    keep_att = pltpu.make_async_copy(att_s[0], att_out.at[pl.ds(0, SEGS[0])], own.at[4])
    keep_dq = pltpu.make_async_copy(dqb_s[0], dq_out.at[pl.ds(0, SEGS[0])], own.at[5])
    keep_att.start()
    back_att.start()
    gate_core.start()

    def backward(seg, b, t):
        kb = k_all[b // 2, pl.ds(t * 2, 2)].reshape(BK, DH)
        vb = v_all[b // 2, pl.ds(t * 2, 2)].reshape(BK, DH)
        slot = bases[seg] + b * UNITS[seg]
        dp = dot(g_s[seg][...], vb, 1, 1)
        delta = d_s[seg][...]
        p = s_s[pl.ds(slot, UNITS[seg])].reshape(STACKS[seg], BK).astype(BF)
        ds = jnp.concatenate(
            [p[:, i : i + DH] * (dp[:, i : i + DH] - delta).astype(BF) for i in range(0, BK, DH)], axis=1
        )
        dq_s[seg][...] += dot(ds, kb, 1, 0)
        dkt_s[t] += dot(qt_s[seg][...], ds, 1, 0)
        dvt_s[t] += dot(gt_s[seg][...], p, 1, 0)

    def write_dq(seg):
        size = SEGS[seg]
        for h in range(GROUP):
            dqb_s[seg][:, h * DH : (h + 1) * DH] = (dq_s[seg][h * size : (h + 1) * size, :] * SCALE).astype(BF)

    def spread_v(n):
        at = (x + n) % NX
        vline_own[n] = dv_part[at, y, c].astype(F32) + core_in[1, n, y].astype(F32)
        for e in range(3):
            to = (y + e + 1) % NY
            vline_out[n, e] = (dv_part[at, to, c].astype(F32) + core_in[1, n, to].astype(F32)).astype(BF)
            line_v(n, e).start()

    def sum_v(n):
        for e in range(3):
            line_v(n, e).wait_recv()
        total = vline_own[n]
        for e in range(3):
            total = total + vline_in[n, e].astype(F32)
        return total

    def gate_step(step):
        @pl.when(step == 0)
        def _():
            gate_core.wait_recv()
            gate_all[0] = gg_s[...] + gate_in[0]
            for copy in gate_across:
                copy.start()

        @pl.when(step == 1)
        def _():
            for copy in gate_across:
                copy.wait_recv()
            gate_all[1] = gate_all[0] + gate_in[1] + gate_in[2] + gate_in[3]
            for copy in gate_along:
                copy.start()

        @pl.when(step == 2)
        def _():
            for copy in gate_along:
                copy.wait_recv()
            total = gate_all[1] + gate_in[4] + gate_in[5] + gate_in[6]
            gate_all[2] = total
            for copy in gate_heads:
                copy.start()

    def pass_on(n):
        pair_k(n).wait_recv()
        group = (x + n) % NX
        kline_out[n - 1] = (dk_part[group, :, c].astype(F32) + core_in[0, n].astype(F32)).astype(BF)
        line_k(n).start()
        pair_v(n).wait_recv()
        spread_v(n)

    def grad_step(step):
        n = (step + 1) % NX
        at = (x + n) % NX
        dkt_s[...] = jnp.zeros((2, DH, BK), F32)
        dvt_s[...] = jnp.zeros((2, DH, BK), F32)

        for seg in (1, 0):

            def block(t):
                b = at * 2 + t
                if seg == 0:
                    pl.when((step > 0) & (t == 1))(lambda: pass_on(step))
                pl.when(b < blocks[seg])(lambda: backward(seg, b, t))

            loop(2, block)
            if seg == 1:

                @pl.when(step == 3)
                def _():
                    write_dq(1)
                    back_dq.start()

        for t in range(2):
            dk_part[at, t * 2 : t * 2 + 2] = (dkt_s[t] * SCALE).T.astype(BF).reshape(2, 2, ROWS, DH)
            dv_part[at, t * 2 : t * 2 + 2] = dvt_s[t].T.astype(BF).reshape(2, 2, ROWS, DH)
        pair_k(n).start()
        pair_v(n).start()
        gate_step(step)

        @pl.when(step > 1)
        def _():
            vlast_out[step - 2] = sum_v(step - 1).astype(BF)
            last_v(step - 1).start()

    loop(4, grad_step)
    write_dq(0)
    keep_dq.start()

    pair_v(0).wait_recv()
    spread_v(0)
    pair_k(0).wait_recv()
    kline_own[...] = dk_part[x, :, c].astype(F32) + core_in[0, 0].astype(F32)
    for n in range(1, 4):
        line_k(n).wait_recv()
    kline_own[...] += kline_in[0].astype(F32) + kline_in[1].astype(F32) + kline_in[2].astype(F32)
    klast_out[...] = kline_own[...].astype(BF)
    for e in range(3):
        last_k(e).start()
    vlast_out[2] = sum_v(3).astype(BF)
    last_v(3).start()
    v_total = sum_v(0)
    k_total = kline_own[y]
    for e in range(3):
        last_k(e).wait_recv()
        k_total = k_total + klast_in[e].astype(F32)
    dk_out[...] = k_total.astype(BF)
    for n in range(1, 4):
        last_v(n).wait_recv()
        v_total = v_total + vlast_in[n - 1].astype(F32)
    dv_out[...] = v_total.astype(BF)
    total = gate_all[2]
    for d in range(NZ - 1):
        gate_heads[d].wait_recv()
        total = total + gate_in[7 + d]
    gg_out[...] = total
    keep_att.wait()
    keep_dq.wait()
    back_att.wait()
    back_dq.wait()
    rows_q.wait_send()
    rows_g.wait_send()
    for d in range(3):
        one_k(d).wait_send()
        one_v(d).wait_send()
        for j in range(4):
            two_k(d, j).wait_send()
            two_v(d, j).wait_send()
        line_k(d + 1).wait_send()
        last_k(d).wait_send()
        last_v(d + 1).wait_send()
    for n in range(4):
        core_k(n).wait_send()
        core_v(n).wait_send()
        pair_k(n).wait_send()
        pair_v(n).wait_send()
        for e in range(3):
            line_v(n, e).wait_send()
    for copy in [gate_core] + gate_across + gate_along + gate_heads:
        copy.wait_send()


def train(flags, sinks, wins, gates, q, g, k, v):
    smem = pl.BlockSpec(memory_space=pltpu.SMEM)
    vmem = pl.BlockSpec(memory_space=pltpu.VMEM)
    anywhere = pl.BlockSpec(memory_space=pl.ANY)
    dma = pltpu.SemaphoreType.DMA
    shape = jax.ShapeDtypeStruct
    hold = pltpu.VMEM
    whole = (NX, NY, 2, ROWS, DH)
    block = (NY, ROWS, DH)
    return pl.pallas_call(
        train_kernel,
        out_shape=(
            shape((ROWS, WIDTH), BF), shape((ROWS, WIDTH), BF), shape((ROWS, DH), BF), shape((ROWS, DH), BF),
            shape((8, DH), F32),
        ),
        in_specs=[smem] * 4 + [anywhere] * 4,
        out_specs=[anywhere] * 2 + [vmem] * 3,
        scratch_shapes=[
            hold(whole, BF), hold(whole, BF),
            *[hold((n, WIDTH), BF) for n in SEGS * 2],
            *[hold(dims, BF) for _ in range(2) for dims in ((STACKS[0], DH), (STACKS[1], DH), (DH, STACKS[0]), (DH, STACKS[1]))],
            *[hold((n, DH), jnp.int32) for n in STACKS * 3],
            *[hold((n, wide), F32) for wide in (DH, 2 * DH, DH, DH) for n in STACKS],
            hold((SLOTS, UNIT, BK), F32), hold((2, DH, BK), F32), hold((2, DH, BK), F32),
            *[hold((n, WIDTH), BF) for n in SEGS * 2], hold((8, DH), F32),
            hold(whole, BF), hold(whole, BF), hold((2, 4) + block, BF),
            hold((3,) + block, BF), hold((3,) + block, BF), hold(block, F32), hold((3, ROWS, DH), BF), hold(block, BF),
            hold((4, 3, ROWS, DH), BF), hold((4, 3, ROWS, DH), BF), hold((4, ROWS, DH), F32),
            hold((3, ROWS, DH), BF), hold((3, ROWS, DH), BF),
            hold((14, 8, DH), F32), hold((3, 8, DH), F32),
            dma((6,)), dma((2, 3)), dma((2, 3)), dma((2, 3, 4)), dma((2, 3, 4)), dma((2, 4)), dma((2, 4)), dma((2,)), dma((2,)),
            dma((2,)), dma((2,)), dma((2, 4)), dma((2, 4)), dma((3,)), dma((3,)), dma((4, 3)), dma((4, 3)),
            dma((2, 3)), dma((2, 3)), dma((14,)), dma((14,)),
        ],
        compiler_params=pltpu.CompilerParams(
            collective_id=0, has_side_effects=True, vmem_limit_bytes=60 * 1024 * 1024
        ),
        name="train",
    )(flags, sinks, wins, gates, q, g, k, v)


def hand_kernel(att_ref, dq_ref, dk_ref, dv_ref, gg_ref, att_out, dq_out, dk_out, dv_out, gg_out, att_s, dq_s, dk_s, dv_s, sems):
    fetched = [
        pltpu.make_async_copy(src, dst, sems.at[n])
        for n, (src, dst) in enumerate(((att_ref, att_s), (dq_ref, dq_s), (dk_ref, dk_s), (dv_ref, dv_s)))
    ]
    stored = [
        pltpu.make_async_copy(src, dst, sems.at[4 + n])
        for n, (src, dst) in enumerate(((att_s, att_out), (dq_s, dq_out), (dk_s, dk_out), (dv_s, dv_out)))
    ]
    for copy in fetched:
        copy.start()
    gg_out[...] = gg_ref[0, : NZ * GROUP]
    for n in range(4):
        fetched[n].wait()
        stored[n].start()
    for copy in stored:
        copy.wait()


def hand(att, dq, dk, dv, gg):
    vmem = pl.BlockSpec(memory_space=pltpu.VMEM)
    anywhere = pl.BlockSpec(memory_space=pl.ANY)
    shape = jax.ShapeDtypeStruct
    return pl.pallas_call(
        hand_kernel,
        out_shape=(
            shape(att.shape, BF), shape(dq.shape, BF), shape(dk.shape, BF), shape(dv.shape, BF), shape((NZ * GROUP,), F32),
        ),
        in_specs=[anywhere] * 4 + [vmem],
        out_specs=[anywhere] * 4 + [vmem],
        scratch_shapes=[*[pltpu.VMEM(part.shape, BF) for part in (att, dq, dk, dv)], pltpu.SemaphoreType.DMA((8,))],
        name="hand",
    )(att, dq, dk, dv, gg)


def local(queries, key_states, value_states, head_gates, retrieval, sink_count, window_len, out_grad):
    return hand(
        *train(retrieval, sink_count, window_len, head_gates, queries, out_grad, key_states, value_states)
    )


def solution(mesh):
    wide = P("ctx", "head")
    return jax.shard_map(
        local,
        mesh=mesh,
        in_specs=(wide, wide, wide, P("head"), P("head"), P("head"), P("head"), wide),
        out_specs=(wide, wide, wide, wide, P()),
        check_vma=False,
    )
```

time: 80.8 us -> 73.2 us (0.906)
  local copies, waits for them, and re-layouts: 5.49 us -> 0 us
  Pallas kernels: 74.3 us -> 72.3 us
    pallas_call x1, Pallas kernels: 74.3 us -> 69.2 us  [train(): pl.pallas_call(train_kernel, out_shape=(shape((ROWS, WIDTH), BF), shape((...]
    unnamed x10 -> x0, local copies, waits for them, and re-layouts: 4.05 us -> none
    pallas_call x0 -> x1, Pallas kernels: none -> 3.14 us  [hand(): pl.pallas_call(hand_kernel, out_shape=(shape(att.shape, BF), shape(dq.sha...]
    slice x1 -> x0, local copies, waits for them, and re-layouts: 0.84 us -> none  [local(): return (att, dq, dk, dv, gg[:, :, 0].reshape(NZ * GROUP))]
where the time goes in v2:
time: 73.2 us; the launch traced here: 72.9 us
  Pallas kernels  72.3 us (99%)
    pallas_call x1, Pallas kernels, train(): pl.pallas_call(train_kernel, out_shape=(shape((ROWS, WIDTH), BF), shape((...  69.2 us
    pallas_call x1, Pallas kernels, hand(): pl.pallas_call(hand_kernel, out_shape=(shape(att.shape, BF), shape(dq.sha...  3.14 us

profile of v2, /device:TPU:2, one launch (start us, length us, event | category | flops | bytes accessed | tf_op | source)
XLA Modules:
  0.0 72.9 jit_solution(10317295638626528334)
XLA Ops:
  0.6 69.2 %train.1 = (bf16[192,1024]{1,0:T(8,128)(2,1)}, bf16[192,1024]{1,0:T(8,128)(2,1)}, bf16[192,128]{1,0:T(8,128)(2,1)}, bf16[192,128]{1,0:T(8,128)(2,1)}, f32[8,128]{1,0:T(8,128)}) custom-call(s32[8]{0:T(128)} %flag_ref.1, s32[8]{0:T(128)} %sink_ref.1, s32[8]{0:T(128)} %win_ref.1, f32[8]{0:T(128)} %gate_ref.1, bf16[192,1024]{1,0:T(8,128)(2,1)} %q_ref.1, ...), custom_call_target="tpu_custom_call" | custom-call | tf_op jit(solution)/shard_map/train/pallas_call | solution.py:464
  69.8 3.1 %hand.1 = (bf16[192,1024]{1,0:T(8,128)(2,1)}, bf16[192,1024]{1,0:T(8,128)(2,1)}, bf16[192,128]{1,0:T(8,128)(2,1)}, bf16[192,128]{1,0:T(8,128)(2,1)}, f32[64]{0:T(128)}) custom-call(bf16[192,1024]{1,0:T(8,128)(2,1)} %get-tuple-element.10.att_ref, bf16[192,1024]{1,0:T(8,128)(2,1)} %get-tuple-element.11.dq_ref, bf16[192,128]{1,0:T(8,128)(2,1)} %get-tuple-element.12.dk_ref, ...), custom_call_target="tpu_custom_call" | custom-call | tf_op jit(solution)/shard_map/hand/pallas_call | solution.py:519
